TPU v7x, 256 devices: a whole 4x4x8 slice. The times are simulated.
256 devices in a mesh: rows: 32 (over z_hi, y, x), cols: 8 (over z_lo, core).
Axes of the slice: x: 4, y: 4, z: 8 (z_hi: 2, z_lo: 4; z = z_hi * 4 + z_lo), core: 2. Of those that a mesh axis runs over, the one named last changes fastest.
Arguments:
- logged: bfloat16 [32768, 256], P(('rows', 'cols')), may hold values from -8 to 8
- fresh: bfloat16 [65536, 256], P(('cols', 'rows')), may hold values from -6 to 6
- warm: float32 [65536], P('cols'), may hold values from -1 to 1
Outputs:
- row_potential: float32 [32768], P('rows')
- col_potential: float32 [65536], P('cols')
- reward: float32 [32768], P('rows')
All inputs are finite; a program needn't handle non-finite values.
Results may differ from a plain program's by a relative error of at most 0.0013.
Values may be sent and summed in bfloat16 or wider, within the bound.
No kernel may reach another device: no remote copies, remote signals or barrier semaphores. Data moves between devices by JAX's collectives and lax.ppermute only.
A program may use at most 128 MiB of HBM per device.

v0:
```python
import jax
import jax.numpy as jnp
from jax import lax
from jax.sharding import PartitionSpec as P

EPS = 0.01


def body(logged, fresh, warm):
    block = lax.all_gather(logged, "cols", axis=0, tiled=True)
    wide = block.astype(jnp.float32)
    block_sq = jnp.sum(wide * wide, axis=1)
    width = block.shape[1]
    total_rows = block.shape[0] * lax.axis_size("rows")
    total_cols = warm.shape[0] * lax.axis_size("cols")
    piece = lax.all_gather(fresh, "rows", axis=0, tiled=True)
    piece_wide = piece.astype(jnp.float32)
    piece_sq = jnp.sum(piece_wide * piece_wide, axis=1)
    inner = lax.dot_general(
        block, piece, (((1,), (1,)), ((), ())), preferred_element_type=jnp.float32
    )
    stored = (block_sq[:, None] + piece_sq[None, :] - 2.0 * inner) / width

    def get_tile():
        return stored

    expo = (warm[None, :] - get_tile()) / EPS
    top = jnp.max(expo, axis=1)
    total = jnp.sum(jnp.exp(expo - top[:, None]), axis=1)
    both = lax.pmax(top, "cols")
    total = lax.psum(total * jnp.exp(top - both), "cols")
    top = both
    row_potential = -EPS * (top + jnp.log(total)) - EPS * jnp.log(jnp.float32(total_rows))
    expo = (row_potential[:, None] - get_tile()) / EPS
    top = jnp.max(expo, axis=0)
    total = jnp.sum(jnp.exp(expo - top[None, :]), axis=0)
    both = lax.pmax(top.astype(jnp.bfloat16), "rows").astype(top.dtype)
    total = lax.psum(total * jnp.exp(top - both), "rows")
    top = both
    col_potential = -EPS * (top + jnp.log(total)) - EPS * jnp.log(jnp.float32(total_cols))
    cost = get_tile()
    plan = jnp.exp((row_potential[:, None] + col_potential[None, :] - cost) / EPS)
    partial_cost = jnp.sum(plan * cost, axis=1)
    reward = -jnp.float32(total_rows) * lax.psum(partial_cost, "cols")
    return (row_potential, col_potential, reward)


def solution(mesh):
    return jax.shard_map(
        body,
        mesh=mesh,
        in_specs=(P(("rows", "cols"), None), P(("cols", "rows"), None), P("cols")),
        out_specs=(P("rows"), P("cols"), P("rows")),
        check_vma=False,
    )
```

profile of v0, /device:TPU:1, one launch (start us, length us, event | category | flops | bytes accessed | tf_op | source)
XLA Modules:
  0.0 682.2 jit_solution(6621677491578648344)
XLA Ops:
  7.2 0.0 all-gather.2.cloned.1.call-start
  7.2 0.7 all-gather.2.cloned.1.call-update
  7.9 18.0 %all_gather.6 = bf16[1024,256]{1,0:T(8,128)(2,1)S(1)} all-gather(bf16[128,256]{1,0:T(8,128)(2,1)} %param.3), channel_id=1, replica_groups=mesh['rows'=32,'cols'=8] {'cols'}, dimensions={0}, use_global_device_ids=true | all-gather | bytes 589824 | tf_op jit(solution)/shard_map/all_gather | solution.py:10
  25.9 0.2 multiply_reduce_fusion.2
  26.1 96.6 %all-gather.2.cloned.1.call-done = bf16[8192,256]{1,0:T(8,128)(2,1)} async-done(((bf16[256,256]{1,0:T(8,128)(2,1)}), bf16[8192,256]{1,0:T(8,128)(2,1)}) %all-gather.2.cloned.1.call-update) | async-done | bytes 4194320 | tf_op jit(solution)/shard_map/all_gather | solution.py:16
  122.7 3.3 multiply_reduce_fusion.1
  126.0 0.0 copy-start.2
  126.1 15.9 %fusion = (f32[1024]{0:T(1024)S(1)}, f32[1024,8192]{1,0:T(8,128)}) fusion(f32[8192]{0:T(1024)} %param.5, bf16[1024,256]{1,0:T(8,128)(2,1)S(1)} %all_gather.6, bf16[8192,256]{1,0:T(8,128)(2,1)} %all-gather.2.cloned.1.call-done, f32[8192]{0:T(1024)S(1)} %multiply_reduce_fusion.1, f32[1024]{0:T(1024)S(1)} %multiply_reduce_fusion.2), kind=kOutput, calls=%fused_computation.6 | convolution fusion | flops 4353686528 | bytes 38346752 | tf_op jit(solution)/shard_map/dot_general | solution.py:19
  142.0 17.9 %pmax.14 = f32[1024]{0:T(1024)S(1)} all-reduce(f32[1024]{0:T(1024)S(1)} %get-tuple-element.3), channel_id=1, replica_groups=mesh['rows'=32,'cols'=8] {'cols'}, use_global_device_ids=true, to_apply=%region_3.0 | all-reduce | flops 1024 | bytes 8192 | tf_op jit(solution)/shard_map/pmax | solution.py:30
  159.9 0.0 copy-done.2
  159.9 14.7 %exponential_reduce_fusion.1 = f32[1024]{0:T(1024)S(1)} fusion(f32[1024,8192]{1,0:T(8,128)} %get-tuple-element.4, f32[1024]{0:T(1024)S(1)} %get-tuple-element.3, f32[8192]{0:T(1024)S(1)} %copy-done.2), kind=kLoop, calls=%fused_computation.3 | loop fusion | flops 33553408 | bytes 33595392 | tf_op jit(solution)/shard_map/reduce_sum | solution.py:29
  174.7 13.6 %psum.21 = f32[1024]{0:T(1024)S(1)} all-reduce(f32[1024]{0:T(1024)S(1)} %exponential_multiply_fusion), channel_id=1, replica_groups=mesh['rows'=32,'cols'=8] {'cols'}, use_global_device_ids=true, to_apply=%region_5.0 | all-reduce | flops 1024 | bytes 8192 | tf_op jit(solution)/shard_map/psum | solution.py:31
  188.3 0.0 copy-start.1
  188.3 12.9 %fusion.1 = f32[8192]{0:T(1024)S(1)} fusion(f32[1024,8192]{1,0:T(8,128)} %get-tuple-element.4, f32[1024]{0:T(1024)S(1)} %multiply_add_fusion), kind=kLoop, calls=%fused_computation.7 | loop fusion | flops 25157632 | bytes 33591296 | tf_op jit(solution)/shard_map/reduce_max | solution.py:35
  201.2 14.5 %exponential_reduce_fusion = f32[8192]{0:T(1024)S(1)} fusion(f32[1024,8192]{1,0:T(8,128)} %get-tuple-element.4, f32[8192]{0:T(1024)S(1)} %fusion.1, f32[1024]{0:T(1024)S(1)} %multiply_add_fusion), kind=kLoop, calls=%fused_computation.1 | loop fusion | flops 33546240 | bytes 33624064 | tf_op jit(solution)/shard_map/reduce_sum | solution.py:36
  215.7 187.5 %pmax.15 = bf16[8192]{0:T(1024)(128)(2,1)S(1)} all-reduce(bf16[8192]{0:T(1024)(128)(2,1)S(1)} %convert_element_type.14), channel_id=1, replica_groups=mesh['rows'=32,'cols'=8] {'rows'}, use_global_device_ids=true, to_apply=%region_7.0 | all-reduce | flops 8192 | bytes 32768 | tf_op jit(solution)/shard_map/pmax | solution.py:37
  403.2 187.1 %psum.22 = f32[8192]{0:T(1024)S(1)} all-reduce(f32[8192]{0:T(1024)S(1)} %fusion.3), channel_id=1, replica_groups=mesh['rows'=32,'cols'=8] {'rows'}, use_global_device_ids=true, to_apply=%region_9.0 | all-reduce | flops 8192 | bytes 65536 | tf_op jit(solution)/shard_map/psum | solution.py:38
  590.4 0.0 copy-done.1
  590.4 0.0 copy-start
  590.4 15.1 %multiply_reduce_fusion = f32[1024]{0:T(1024)S(1)} fusion(f32[1024,8192]{1,0:T(8,128)} %get-tuple-element.4, f32[8192]{0:T(1024)S(1)} %fusion.5, f32[1024]{0:T(1024)S(1)} %multiply_add_fusion), kind=kLoop, calls=%fused_computation | loop fusion | flops 41942016 | bytes 33595392 | tf_op jit(solution)/shard_map/reduce_sum | solution.py:43
  605.5 69.3 %psum.23 = f32[1024]{0:T(1024)S(1)} all-reduce(f32[1024]{0:T(1024)S(1)} %multiply_reduce_fusion), channel_id=1, replica_groups=mesh['rows'=32,'cols'=8] {'cols'}, use_global_device_ids=true, to_apply=%region_11.0 | all-reduce | flops 1024 | bytes 8192 | tf_op jit(solution)/shard_map/psum | solution.py:44
  674.7 0.6 broadcast_multiply_fusion
  675.3 0.0 copy-done
  (5 shorter events, 0.1 us)
Async XLA Ops:
  7.2 115.5 %all-gather.2.cloned.1.call-start = ((), (), s32[]{:S(2)}) async-start(), calls=%async_computation | async-start | bytes 4325376 | tf_op jit(solution)/shard_map/all_gather | solution.py:16
  126.0 33.9 %copy-start.2 = (f32[8192]{0:T(1024)S(1)}, f32[8192]{0:T(1024)}, u32[]{:S(2)}) copy-start(f32[8192]{0:T(1024)} %param.5) | copy-start | bytes 98308
  188.3 402.1 %copy-start.1 = (f32[1024]{0:T(1024)}, f32[1024]{0:T(1024)S(1)}, u32[]{:S(2)}) copy-start(f32[1024]{0:T(1024)S(1)} %multiply_add_fusion) | copy-start | bytes 12292
  590.4 85.0 %copy-start = (f32[8192]{0:T(1024)}, f32[8192]{0:T(1024)S(1)}, u32[]{:S(2)}) copy-start(f32[8192]{0:T(1024)S(1)} %fusion.5) | copy-start | bytes 98308
Sparse Core Ops, SparseCore 0:
  11.4 111.2 all-gather.1
where the time goes:
time: 683 us; the launch traced here: 682 us
  blocking collectives  493 us (72%)
  waiting for transfers between devices  97.3 us (14%)
  other arithmetic  61.4 us (9%)
  matrix products  15.9 us (2%)
  between operations  14.1 us (2%)
    pmax x1, blocking collectives, body(): both = lax.pmax(top.astype(jnp.bfloat16), 'rows').astype(top.dtype)  188 us
    psum x1, blocking collectives, body(): total = lax.psum(total * jnp.exp(top - both), 'rows')  187 us
    all_gather x1, waiting for transfers between devices, body(): piece = lax.all_gather(fresh, 'rows', axis=0, tiled=True)  96.6 us
    psum x1, blocking collectives, body(): reward = -jnp.float32(total_rows) * lax.psum(partial_cost, 'cols')  69.3 us
    all_gather x1, blocking collectives, body(): block = lax.all_gather(logged, 'cols', axis=0, tiled=True)  18 us
    pmax x1, blocking collectives, body(): both = lax.pmax(top, 'cols')  17.9 us
    dot_general x1, matrix products, body(): lax.dot_general(block, piece, (((1,), (1,)), ((), ())), preferred_element...  15.9 us
    reduce_sum x1, other arithmetic, body(): partial_cost = jnp.sum(plan * cost, axis=1)  15.1 us
  transfers between devices with their start and end apart: 1, of which 1 were waited for; matrix products, arithmetic and copies ran while one was open for 0% of the time, Pallas kernels for 0%

commit v1 on v0

--- a/solution.py
+++ b/solution.py
@@ -1,9 +1,18 @@
+import functools
 import jax
 import jax.numpy as jnp
 from jax import lax
 from jax.sharding import PartitionSpec as P
 
 EPS = 0.01
+
+
+def switch_the_keys(block_here, ax_name):
+    left_arr = lax.all_gather(block_here, ax_name)
+    return jnp.sum(left_arr, 0)
+
+
+_handle_spans = functools.partial(switch_the_keys, ax_name="rows")
 
 
 def body(logged, fresh, warm):
@@ -35,7 +44,7 @@
     top = jnp.max(expo, axis=0)
     total = jnp.sum(jnp.exp(expo - top[None, :]), axis=0)
     both = lax.pmax(top.astype(jnp.bfloat16), "rows").astype(top.dtype)
-    total = lax.psum(total * jnp.exp(top - both), "rows")
+    total = _handle_spans(total * jnp.exp(top - both))
     top = both
     col_potential = -EPS * (top + jnp.log(total)) - EPS * jnp.log(jnp.float32(total_cols))
     cost = get_tile()

time: 683 us -> 550 us (0.81)
  blocking collectives: 493 us -> 252 us
  waiting for transfers between devices: 97.3 us -> 203 us
    psum x1 -> x0, blocking collectives: 187 us -> none  [body(): total = lax.psum(total * jnp.exp(top - both), 'rows')]
    all_gather x0 -> x1, waiting for transfers between devices: none -> 106 us  [switch_the_keys(): left_arr = lax.all_gather(block_here, ax_name)]
    psum x1, blocking collectives: 69.3 us -> 15.2 us  [body(): reward = -jnp.float32(total_rows) * lax.psum(partial_cost, 'cols')]
  transfers between devices with their start and end apart: 1 -> 2, of which waited for: 1 -> 2; matrix products, arithmetic and copies ran while one was open for 0% -> 0% of each run, Pallas kernels for 0% -> 0%
where the time goes in v1:
time: 550 us; the launch traced here: 549 us
  blocking collectives  252 us (46%)
  waiting for transfers between devices  203 us (37%)
  other arithmetic  62.1 us (11%)
  matrix products  15.9 us (3%)
  between operations  14.1 us (3%)
    pmax x1, blocking collectives, body(): both = lax.pmax(top.astype(jnp.bfloat16), 'rows').astype(top.dtype)  188 us
    all_gather x1, waiting for transfers between devices, switch_the_keys(): left_arr = lax.all_gather(block_here, ax_name)  106 us
    all_gather x1, waiting for transfers between devices, body(): piece = lax.all_gather(fresh, 'rows', axis=0, tiled=True)  96.6 us
    all_gather x1, blocking collectives, body(): block = lax.all_gather(logged, 'cols', axis=0, tiled=True)  18 us
    pmax x1, blocking collectives, body(): both = lax.pmax(top, 'cols')  17.9 us
    dot_general x1, matrix products, body(): lax.dot_general(block, piece, (((1,), (1,)), ((), ())), preferred_element...  15.9 us
    psum x1, blocking collectives, body(): reward = -jnp.float32(total_rows) * lax.psum(partial_cost, 'cols')  15.2 us
    reduce_sum x1, other arithmetic, body(): partial_cost = jnp.sum(plan * cost, axis=1)  15.1 us
  transfers between devices with their start and end apart: 2, of which 2 were waited for; matrix products, arithmetic and copies ran while one was open for 0% of the time, Pallas kernels for 0%

profile of v1, /device:TPU:1, one launch (start us, length us, event | category | flops | bytes accessed | tf_op | source)
XLA Modules:
  0.0 549.4 jit_solution(879036243989912328)
XLA Ops:
  7.2 0.0 all-gather.4.cloned.1.call-start
  7.2 0.7 all-gather.4.cloned.1.call-update
  7.9 0.0 all-gather.6.cloned.1.call-start
  7.9 18.0 %all_gather.12 = bf16[1024,256]{1,0:T(8,128)(2,1)S(1)} all-gather(bf16[128,256]{1,0:T(8,128)(2,1)} %param.3), channel_id=1, replica_groups=mesh['rows'=32,'cols'=8] {'cols'}, dimensions={0}, use_global_device_ids=true | all-gather | bytes 589824 | tf_op jit(solution)/shard_map/all_gather | solution.py:19
  25.9 0.2 multiply_reduce_fusion.2
  26.1 96.6 %all-gather.4.cloned.1.call-done = bf16[8192,256]{1,0:T(8,128)(2,1)} async-done(((bf16[256,256]{1,0:T(8,128)(2,1)}), bf16[8192,256]{1,0:T(8,128)(2,1)}) %all-gather.4.cloned.1.call-update) | async-done | bytes 4194320 | tf_op jit(solution)/shard_map/all_gather | solution.py:25
  122.7 3.3 multiply_reduce_fusion.1
  126.0 0.0 copy-start.2
  126.1 15.9 %fusion = (f32[1024]{0:T(1024)S(1)}, f32[1024,8192]{1,0:T(8,128)}) fusion(f32[8192]{0:T(1024)} %param.5, bf16[1024,256]{1,0:T(8,128)(2,1)S(1)} %all_gather.12, bf16[8192,256]{1,0:T(8,128)(2,1)} %all-gather.4.cloned.1.call-done, f32[8192]{0:T(1024)S(1)} %multiply_reduce_fusion.1, f32[1024]{0:T(1024)S(1)} %multiply_reduce_fusion.2), kind=kOutput, calls=%fused_computation.6 | convolution fusion | flops 4353686528 | bytes 38346752 | tf_op jit(solution)/shard_map/dot_general | solution.py:28
  142.0 17.9 %pmax.14 = f32[1024]{0:T(1024)S(1)} all-reduce(f32[1024]{0:T(1024)S(1)} %get-tuple-element.3), channel_id=1, replica_groups=mesh['rows'=32,'cols'=8] {'cols'}, use_global_device_ids=true, to_apply=%region_3.0 | all-reduce | flops 1024 | bytes 8192 | tf_op jit(solution)/shard_map/pmax | solution.py:39
  159.9 0.0 copy-done.2
  159.9 14.7 %exponential_reduce_fusion.1 = f32[1024]{0:T(1024)S(1)} fusion(f32[1024,8192]{1,0:T(8,128)} %get-tuple-element.4, f32[1024]{0:T(1024)S(1)} %get-tuple-element.3, f32[8192]{0:T(1024)S(1)} %copy-done.2), kind=kLoop, calls=%fused_computation.3 | loop fusion | flops 33553408 | bytes 33595392 | tf_op jit(solution)/shard_map/reduce_sum | solution.py:38
  174.7 13.6 %psum.14 = f32[1024]{0:T(1024)S(1)} all-reduce(f32[1024]{0:T(1024)S(1)} %exponential_multiply_fusion), channel_id=1, replica_groups=mesh['rows'=32,'cols'=8] {'cols'}, use_global_device_ids=true, to_apply=%region_5.0 | all-reduce | flops 1024 | bytes 8192 | tf_op jit(solution)/shard_map/psum | solution.py:40
  188.3 0.0 copy-start.1
  188.3 12.9 %fusion.1 = f32[8192]{0:T(1024)S(1)} fusion(f32[1024,8192]{1,0:T(8,128)} %get-tuple-element.4, f32[1024]{0:T(1024)S(1)} %multiply_add_fusion), kind=kLoop, calls=%fused_computation.7 | loop fusion | flops 25157632 | bytes 33591296 | tf_op jit(solution)/shard_map/reduce_max | solution.py:44
  201.2 14.5 %exponential_reduce_fusion = f32[8192]{0:T(1024)S(1)} fusion(f32[1024,8192]{1,0:T(8,128)} %get-tuple-element.4, f32[8192]{0:T(1024)S(1)} %fusion.1, f32[1024]{0:T(1024)S(1)} %multiply_add_fusion), kind=kLoop, calls=%fused_computation.1 | loop fusion | flops 33546240 | bytes 33624064 | tf_op jit(solution)/shard_map/reduce_sum | solution.py:45
  215.7 187.5 %pmax.15 = bf16[8192]{0:T(1024)(128)(2,1)S(1)} all-reduce(bf16[8192]{0:T(1024)(128)(2,1)S(1)} %convert_element_type.14), channel_id=1, replica_groups=mesh['rows'=32,'cols'=8] {'rows'}, use_global_device_ids=true, to_apply=%region_7.0 | all-reduce | flops 8192 | bytes 32768 | tf_op jit(solution)/shard_map/pmax | solution.py:46
  403.2 0.6 fusion.3
  403.9 0.0 all-gather.6.cloned.1.call-update
  403.9 106.2 %all-gather.6.cloned.1.call-done = f32[262144]{0:T(1024)} async-done(((f32[8192]{0:T(1024)}), f32[262144]{0:T(1024)}) %all-gather.6.cloned.1.call-update) | async-done | bytes 1048592 | tf_op jit(solution)/shard_map/all_gather | solution.py:11
  510.1 1.4 reshape.13
  511.5 0.1 reduce_sum.58
  511.6 0.0 copy-done.1
  511.6 0.0 copy-start
  511.7 15.1 %multiply_reduce_fusion = f32[1024]{0:T(1024)S(1)} fusion(f32[1024,8192]{1,0:T(8,128)} %get-tuple-element.4, f32[8192]{0:T(1024)S(1)} %fusion.5, f32[1024]{0:T(1024)S(1)} %multiply_add_fusion), kind=kLoop, calls=%fused_computation | loop fusion | flops 41942016 | bytes 33595392 | tf_op jit(solution)/shard_map/reduce_sum | solution.py:52
  526.7 15.2 %psum.15 = f32[1024]{0:T(1024)S(1)} all-reduce(f32[1024]{0:T(1024)S(1)} %multiply_reduce_fusion), channel_id=1, replica_groups=mesh['rows'=32,'cols'=8] {'cols'}, use_global_device_ids=true, to_apply=%region_11.0 | all-reduce | flops 1024 | bytes 8192 | tf_op jit(solution)/shard_map/psum | solution.py:53
  542.0 0.6 broadcast_multiply_fusion
  542.6 0.0 copy-done
  (4 shorter events, 0.0 us)
Async XLA Ops:
  7.2 115.5 %all-gather.4.cloned.1.call-start = ((), (), s32[]{:S(2)}) async-start(), calls=%async_computation | async-start | bytes 4325376 | tf_op jit(solution)/shard_map/all_gather | solution.py:25
  7.9 502.2 %all-gather.6.cloned.1.call-start = ((), (), s32[]{:S(2)}) async-start(), calls=%async_computation.1 | async-start | bytes 1081344 | tf_op jit(solution)/shard_map/all_gather | solution.py:11
  126.0 33.9 %copy-start.2 = (f32[8192]{0:T(1024)S(1)}, f32[8192]{0:T(1024)}, u32[]{:S(2)}) copy-start(f32[8192]{0:T(1024)} %param.5) | copy-start | bytes 98308
  188.3 323.4 %copy-start.1 = (f32[1024]{0:T(1024)}, f32[1024]{0:T(1024)S(1)}, u32[]{:S(2)}) copy-start(f32[1024]{0:T(1024)S(1)} %multiply_add_fusion) | copy-start | bytes 12292
  511.6 30.9 %copy-start = (f32[8192]{0:T(1024)}, f32[8192]{0:T(1024)S(1)}, u32[]{:S(2)}) copy-start(f32[8192]{0:T(1024)S(1)} %fusion.5) | copy-start | bytes 98308
Sparse Core Ops, SparseCore 0:
  11.4 111.2 all-gather.3
  404.0 106.0 all-gather.5
